TPU v7x, 512 devices: a whole 4x4x16 slice. The times are simulated.
512 devices in a mesh: blk: 16 (over y_hi, x, core), dp: 32 (over y_lo, z).
Axes of the slice: x: 4, y: 4 (y_hi: 2, y_lo: 2; y = y_hi * 2 + y_lo), z: 16, core: 2. Of those that a mesh axis runs over, the one named last changes fastest.
Arguments:
- queries: bfloat16 [32, 1024, 3584], P('dp', 'blk'), may hold values from -0.33407655 to 0.33407655
- passages: bfloat16 [32, 1024, 3584], P('dp', 'blk'), may hold values from -0.10022297 to 0.10022297
- positive: int32 [32, 1024], P('dp'), may hold values from 0 to 1023, as said below
- hard_owner: int32 [32, 1024, 1], P('dp', 'blk'), may hold values from 0 to 31, as said below
- hard_slot: int32 [32, 1024, 1], P('dp', 'blk'), may hold values from 0 to 63
Outputs:
- losses: float32 [32, 1024], P('dp', 'blk')
- question_derivative: bfloat16 [32, 1024, 3584], P('dp', 'blk')
- passage_grad: bfloat16 [32, 1024, 3584], P('dp', 'blk')
Inputs may be any that keep to these rules, and one draw needn't show every extreme that they name: `positive`: in each group the entries are a permutation of 0 to 1023. `hard_owner`: the rows of one device name each group at most 3 times, and one group exactly 3 times.
All inputs are finite; a program needn't handle non-finite values.
Results may differ from a plain program's by a relative error of at most 0.006.
Values may be sent and summed in bfloat16 or wider, within the bound.
A program may use at most 128 MiB of HBM per device.

v0:
```python
import jax
import jax.numpy as jnp
from jax import lax
from jax.sharding import PartitionSpec as P

logit_scale_factor = 50.0


def return_terms(outgoing):
    return lax.all_to_all(outgoing, "dp", split_axis=0, concat_axis=0, tiled=True)


def shards(queries, passages, positive, hard_owner, hard_slot):
    question_embedding_table = queries[0]
    document_embedding_table = passages[0]
    positive_all = positive[0]
    rows_here, width = question_embedding_table.shape
    hard_count = hard_owner.shape[2]
    owner_index = hard_owner[0].reshape(-1)
    slot_rows = hard_slot[0].reshape(-1)
    shard_count = lax.axis_size("dp")
    capacity = max(2, min(rows_here * hard_count, 3 * rows_here * hard_count // (2 * shard_count)))
    offset_rows = lax.axis_index("blk") * rows_here
    positive_here = lax.dynamic_slice_in_dim(positive_all, offset_rows, rows_here)
    group_rows = positive_all.shape[0]
    inverse = (
        jnp.zeros((group_rows,), jnp.int32)
        .at[positive_all]
        .set(jnp.arange(group_rows, dtype=jnp.int32))
    )
    inverse_here = lax.dynamic_slice_in_dim(inverse, offset_rows, rows_here)
    marked = (owner_index[:, None] == jnp.arange(shard_count, dtype=jnp.int32)[None, :]).astype(
        jnp.int32
    )
    places = jnp.sum((jnp.cumsum(marked, 0) - marked) * marked, 1)
    requests = jnp.zeros((shard_count, capacity), jnp.int32).at[owner_index, places].set(slot_rows)
    wanted_rows = lax.all_to_all(requests, "dp", split_axis=0, concat_axis=0, tiled=True)
    fetched = jnp.take(document_embedding_table, wanted_rows.reshape(-1), axis=0).reshape(
        shard_count, capacity, width
    )
    returned = lax.all_to_all(fetched, "dp", split_axis=0, concat_axis=0, tiled=True)
    distractor_documents = returned[owner_index, places].reshape(rows_here, hard_count, width)
    fetched_distractor_logits = logit_scale_factor * jnp.einsum(
        "rd,rhd->rh",
        question_embedding_table,
        distractor_documents,
        preferred_element_type=jnp.float32,
    )
    peak_start = jnp.max(fetched_distractor_logits, 1)
    hard_exp = jnp.exp(fetched_distractor_logits - peak_start[:, None])
    accum_start = jnp.einsum(
        "rh,rhd->rd",
        hard_exp,
        distractor_documents.astype(jnp.float32),
        precision=lax.Precision.HIGHEST,
    )
    segment = lax.all_gather(document_embedding_table, "blk", axis=0, tiled=True)
    aggregate_objective = jnp.sum(hard_exp, 1)
    grand_objective_tally = accum_start
    length = segment.shape[0]
    cosine_logit_table = logit_scale_factor * lax.dot_general(
        question_embedding_table,
        segment,
        (((1,), (1,)), ((), ())),
        preferred_element_type=jnp.float32,
    )
    peak_next = jnp.maximum(peak_start, jnp.max(cosine_logit_table, 1))
    decay = jnp.exp(peak_start - peak_next)
    weights = jnp.exp(cosine_logit_table - peak_next[:, None])
    widened = segment.astype(jnp.float32)
    grand_objective_tally = grand_objective_tally * decay[:, None] + jnp.dot(
        weights, widened, precision=lax.Precision.HIGHEST
    )
    aggregate_objective = aggregate_objective * decay + jnp.sum(weights, 1)
    offsets = positive_here
    inside = (offsets >= 0) & (offsets < length)
    clipped = jnp.clip(offsets, 0, length - 1)
    paired_target_logits = jnp.where(inside[:, None], widened[clipped], 0.0)
    picked = jnp.where(
        inside, jnp.take_along_axis(cosine_logit_table, clipped[:, None], 1)[:, 0], 0.0
    )
    lse_here = peak_next + jnp.log(aggregate_objective)
    losses = lse_here - picked
    question_derivative = (
        logit_scale_factor * (grand_objective_tally / aggregate_objective[:, None])
        - logit_scale_factor * paired_target_logits
    ).astype(jnp.bfloat16)
    distractor_attention_shares = jnp.exp(fetched_distractor_logits - lse_here[:, None])
    distractor_contributions = (
        logit_scale_factor
        * distractor_attention_shares[:, :, None]
        * question_embedding_table.astype(jnp.float32)[:, None, :]
    ).astype(jnp.bfloat16)
    outgoing = (
        jnp.zeros((shard_count, capacity, width), jnp.bfloat16)
        .at[owner_index, places]
        .set(distractor_contributions.reshape(rows_here * hard_count, width))
    )
    lse_group = lax.all_gather(lse_here, "blk", axis=0, tiled=True)
    segment = lax.all_gather(question_embedding_table, "blk", axis=0, tiled=True)
    length = segment.shape[0]
    cosine_logit_table = logit_scale_factor * lax.dot_general(
        segment,
        document_embedding_table,
        (((1,), (1,)), ((), ())),
        preferred_element_type=jnp.float32,
    )
    normalized_exponential_shares = jnp.exp(cosine_logit_table - lse_group[:, None]).astype(
        jnp.bfloat16
    )
    cumulative_partial_value = logit_scale_factor * lax.dot_general(
        normalized_exponential_shares,
        segment,
        (((0,), (0,)), ((), ())),
        preferred_element_type=jnp.float32,
    )
    offsets = inverse_here
    inside = (offsets >= 0) & (offsets < length)
    clipped = jnp.clip(offsets, 0, length - 1)
    within_minibatch_derivative = cumulative_partial_value - logit_scale_factor * jnp.where(
        inside[:, None], segment[clipped].astype(jnp.float32), 0.0
    )
    incoming = return_terms(outgoing)
    owner_rows = (
        wanted_rows.reshape(-1)[None, :] == jnp.arange(rows_here, dtype=jnp.int32)[:, None]
    ).astype(jnp.bfloat16)
    hard_grad = jnp.dot(
        owner_rows,
        incoming.reshape(shard_count * capacity, width),
        preferred_element_type=jnp.float32,
    )
    passage_grad = (within_minibatch_derivative + hard_grad).astype(jnp.bfloat16)
    return (losses[None], question_derivative[None], passage_grad[None])


def solution(mesh):
    placed = (
        P("dp", "blk", None),
        P("dp", "blk", None),
        P("dp", None),
        P("dp", "blk", None),
        P("dp", "blk", None),
    )
    return jax.shard_map(
        shards,
        mesh=mesh,
        in_specs=placed,
        out_specs=(P("dp", "blk"), P("dp", "blk", None), P("dp", "blk", None)),
        check_vma=False,
    )
```

profile of v0, /device:TPU:1, one launch (start us, length us, event | category | flops | bytes accessed | tf_op | source)
XLA Modules:
  0.0 262.8 jit_solution(9674383049980327253)
XLA Ops:
  7.2 0.0 copy-start.2
  7.2 0.0 all-gather.5.cloned.1.call-start
  7.2 0.7 all-gather.5.cloned.1.call-update
  7.9 0.0 all-gather.7.cloned.1.call-start
  8.0 0.7 all-gather.7.cloned.1.call-update
  8.7 0.7 fusion.39
  9.4 0.1 reduce_window_sum.11
  9.5 0.8 select_reduce_fusion
  10.3 0.7 fusion.47
  11.0 5.8 %scatter_fusion = s32[32,3]{0,1:T(4,128)S(1)} fusion(s32[32,3]{0,1:T(4,128)S(1)} %broadcast_in_dim.73, s32[64]{0:T(128)S(1)} %get-tuple-element.8, s32[64]{0:T(128)} %bitcast.99), kind=kCustom, calls=%fused_computation.5 | custom fusion | bytes 1280 | tf_op jit(solution)/shard_map/scatter | solution.py:36
  16.8 0.1 copy.15
  16.8 29.0 %all_to_all.19 = s32[32,1,3]{2,1,0:T(1,128)S(1)} all-to-all(s32[32,1,3]{2,1,0:T(1,128)S(1)} %copy.15), channel_id=1, replica_groups=mesh['blk'=16,'dp'=32] {'dp'}, dimensions={0} | all-to-all | bytes 768 | tf_op jit(solution)/shard_map/all_to_all | solution.py:37
  45.9 0.5 broadcast.423
  46.4 0.7 reduce.7
  47.1 0.1 reshape.287
  47.2 0.0 copy-start.1
  47.2 2.8 %gather_fusion = bf16[96,3584]{1,0:T(8,128)(2,1)S(1)} fusion(bf16[64,3584]{1,0:T(8,128)(2,1)} %bitcast.92, s32[1024]{0:T(1024)S(1)} %pad_clamp_fusion.2), kind=kCustom, calls=%fused_computation | custom fusion | bytes 1376640 | tf_op jit(solution)/shard_map/jit(_take)/gather | solution.py:38
  50.0 0.4 gather.22
  50.4 0.1 copy.16
  50.5 0.1 copy.17
  50.6 1.4 broadcast_select_fusion
  52.0 3.9 %all-to-all-start.1 = ((bf16[32,3,3584]{2,1,0:T(4,128)(2,1)}), bf16[32,3,3584]{2,1,0:T(4,128)(2,1)S(1)}, u32[]{:S(2)}, u32[]{:S(2)}) async-start(bf16[32,3,3584]{2,1,0:T(4,128)(2,1)} %broadcast_select_fusion), calls=%async_computation.1 | async-start | bytes 1835008 | tf_op jit(solution)/shard_map/all_to_all | solution.py:41
  56.0 1.3 dynamic-slice.1
  57.9 0.0 copy-done.2
  57.9 4.3 %scatter_custom_fusion.1 = s32[1024]{0:T(1024)S(1)} fusion(s32[1024]{0:T(1024)S(1)} %bitcast.98, s32[1024]{0:T(1024)S(1)} %iota.11, s32[]{:T(128)} %constant.18.clone.1), kind=kCustom, calls=%fused_computation.59 | custom fusion | bytes 4100 | tf_op jit(solution)/shard_map/scatter | solution.py:29
  62.3 0.1 fusion.52
  62.3 0.1 compare_select_fusion.2
  62.4 0.1 compare_and_fusion
  62.6 0.1 reshape.288
  62.7 38.1 %all-to-all-done.1 = bf16[32,3,3584]{2,1,0:T(4,128)(2,1)S(1)} async-done(((bf16[32,3,3584]{2,1,0:T(4,128)(2,1)}), bf16[32,3,3584]{2,1,0:T(4,128)(2,1)S(1)}, u32[]{:S(2)}, u32[]{:S(2)}) %all-to-all-start.1) | async-done | bytes 688160 | tf_op jit(solution)/shard_map/all_to_all | solution.py:41
  100.8 0.1 copy.18
  101.0 2.0 gather_fusion.1
  103.0 0.0 copy-done.1
  103.0 0.2 fusion.32
  103.2 3.6 %all-gather.5.cloned.1.call-done = bf16[1,1024,3584]{2,1,0:T(8,128)(2,1)} async-done(((bf16[1,64,3584]{2,1,0:T(8,128)(2,1)}), bf16[1,1024,3584]{2,1,0:T(8,128)(2,1)}) %all-gather.5.cloned.1.call-update) | async-done | bytes 7340048 | tf_op jit(solution)/shard_map/all_gather | solution.py:57
  106.8 5.5 %fusion.57 = (f32[64]{0:T(128)S(1)}, f32[64,1024]{1,0:T(8,128)S(1)}) fusion(bf16[1,1024,3584]{2,1,0:T(8,128)(2,1)} %all-gather.5.cloned.1.call-done, bf16[1,64,3584]{2,1,0:T(8,128)(2,1)S(1)} %copy-done.1), kind=kOutput, calls=%fused_computation.90 | convolution fusion | flops 469893056 | bytes 8061184 | tf_op jit(solution)/shard_map/dot_general | solution.py:61
  112.3 0.2 fusion.35
  112.6 0.2 fusion.31
  112.8 9.0 %scatter_fusion.1 = bf16[32,3,3584]{2,0,1:T(8,128)(2,1)S(1)} fusion(bf16[32,3,3584]{2,0,1:T(8,128)(2,1)S(1)} %broadcast_in_dim.83, s32[64]{0:T(128)S(1)} %get-tuple-element.8, bf16[64,3584]{1,0:T(8,128)(2,1)S(1)} %fusion.31), kind=kCustom, calls=%fused_computation.7 | custom fusion | bytes 1376768 | tf_op jit(solution)/shard_map/scatter | solution.py:97
  121.8 1.5 copy.19
  123.3 13.8 %all-to-all-start.2 = ((bf16[32,3,3584]{2,1,0:T(4,128)(2,1)}), bf16[32,3,3584]{2,1,0:T(4,128)(2,1)}, u32[]{:S(2)}, u32[]{:S(2)}) async-start(bf16[32,3,3584]{2,1,0:T(4,128)(2,1)} %copy.19), calls=%async_computation.2 | async-start | bytes 1835008 | tf_op jit(solution)/shard_map/all_to_all | solution.py:10
  137.1 10.4 %bitcast_convert_fusion = f32[1024,3584]{1,0:T(8,128)} fusion(bf16[1,1024,3584]{2,1,0:T(8,128)(2,1)} %all-gather.5.cloned.1.call-done), kind=kLoop, calls=%fused_computation.8 | loop fusion | flops 3670016 | bytes 22020096 | tf_op jit(solution)/shard_map/convert_element_type | solution.py:70
  147.5 0.9 gather_fusion.4
  148.4 6.5 %gather_fusion.2 = f32[64,3584]{1,0:T(8,128)S(1)} fusion(f32[1024,3584]{1,0:T(8,128)} %bitcast_convert_fusion, s32[1024]{0:T(1024)S(1)} %pad_clamp_fusion.1), kind=kCustom, calls=%fused_computation.2 | custom fusion | bytes 1835264 | tf_op jit(solution)/shard_map/gather | solution.py:78
  154.8 42.7 %all-gather.7.cloned.1.call-done = bf16[1,1024,3584]{2,1,0:T(8,128)(2,1)} async-done(((bf16[1,64,3584]{2,1,0:T(8,128)(2,1)}), bf16[1,1024,3584]{2,1,0:T(8,128)(2,1)}) %all-gather.7.cloned.1.call-update) | async-done | bytes 7340048 | tf_op jit(solution)/shard_map/all_gather | solution.py:100
  197.5 5.3 %gather_fusion.3 = bf16[64,3584]{1,0:T(8,128)(2,1)S(1)} fusion(bf16[1024,3584]{1,0:T(8,128)(2,1)} %bitcast.93, s32[1024]{0:T(1024)S(1)} %pad_clamp_fusion), kind=kCustom, calls=%fused_computation.3 | custom fusion | bytes 917760 | tf_op jit(solution)/shard_map/gather | solution.py:121
  202.8 0.1 fusion.55
  203.0 32.8 %all-reduce = f32[1024]{0:T(1024)S(1)} all-reduce(f32[1024]{0:T(1024)S(1)} %fusion.55), channel_id=1, replica_groups=mesh['blk'=16,'dp'=32] {'blk'}, use_global_device_ids=true, to_apply=%add | all-reduce | flops 1024 | bytes 8192
  235.7 0.5 bitcast_subtract_fusion
  236.2 0.0 copy-start
  236.2 8.0 %fusion.21 = bf16[1,64,3584]{2,1,0:T(8,128)(2,1)} fusion(bf16[1,1024,3584]{2,1,0:T(8,128)(2,1)} %all-gather.5.cloned.1.call-done, bf16[64,3584]{1,0:T(8,128)(2,1)S(1)} %gather_fusion.1, f32[64,3584]{1,0:T(8,128)S(1)} %gather_fusion.2, f32[64]{0:T(128)S(1)} %get-tuple-element.4, f32[64]{0:T(128)S(1)} %get-tuple-element.5, f32[64]{0:T(128)S(1)} %get-tuple-element.10, ...), kind=kOutput, calls=%fused_computation.22 | convolution fusion | flops 2820931584 | bytes 9438272 | tf_op jit(solution)/shard_map/dot_general | solution.py:71
  244.3 0.0 copy-done
  244.3 9.0 %fusion.4 = f32[64,3584]{1,0:T(8,128)S(1)} fusion(bf16[64,3584]{1,0:T(8,128)(2,1)S(1)} %gather_fusion.3, pred[64]{0:T(512)(128)(4,1)S(1)} %compare_and_fusion, f32[1024]{0:T(1024)S(1)} %all-reduce, bf16[1,1024,3584]{2,1,0:T(8,128)(2,1)} %all-gather.7.cloned.1.call-done, bf16[1,64,3584]{2,1,0:T(8,128)(2,1)S(1)} %copy-done), kind=kOutput, calls=%fused_computation.15 | convolution fusion | flops 940867584 | bytes 9179200 | tf_op jit(solution)/shard_map/dot_general | solution.py:111
  253.3 0.0 all-to-all-done.2
  253.3 1.6 reshape.289
  254.9 1.0 fusion.24
  (17 shorter events, 0.2 us)
Async XLA Ops:
  7.2 50.7 %copy-start.2 = (s32[1,1024]{1,0:T(1,128)S(1)}, s32[1,1024]{1,0:T(1,128)}, u32[]{:S(2)}) copy-start(s32[1,1024]{1,0:T(1,128)} %param.7) | copy-start | bytes 12292
  7.2 99.7 %all-gather.5.cloned.1.call-start = ((), (), s32[]{:S(2)}) async-start(), calls=%async_computation.3 | async-start | bytes 7798784 | tf_op jit(solution)/shard_map/all_gather | solution.py:57
  7.9 189.6 %all-gather.7.cloned.1.call-start = ((), (), s32[]{:S(2)}) async-start(), calls=%async_computation.4 | async-start | bytes 7798784 | tf_op jit(solution)/shard_map/all_gather | solution.py:100
  47.2 55.8 %copy-start.1 = (bf16[1,64,3584]{2,1,0:T(8,128)(2,1)S(1)}, bf16[1,64,3584]{2,1,0:T(8,128)(2,1)}, u32[]{:S(2)}) copy-start(bf16[1,64,3584]{2,1,0:T(8,128)(2,1)} %param.5) | copy-start | bytes 1376260
  52.0 48.8 %all-to-all-start.1 = ((bf16[32,3,3584]{2,1,0:T(4,128)(2,1)}), bf16[32,3,3584]{2,1,0:T(4,128)(2,1)S(1)}, u32[]{:S(2)}, u32[]{:S(2)}) async-start(bf16[32,3,3584]{2,1,0:T(4,128)(2,1)} %broadcast_select_fusion), calls=%async_computation.1 | async-start | bytes 1835008 | tf_op jit(solution)/shard_map/all_to_all | solution.py:41
  123.3 130.0 %all-to-all-start.2 = ((bf16[32,3,3584]{2,1,0:T(4,128)(2,1)}), bf16[32,3,3584]{2,1,0:T(4,128)(2,1)}, u32[]{:S(2)}, u32[]{:S(2)}) async-start(bf16[32,3,3584]{2,1,0:T(4,128)(2,1)} %copy.19), calls=%async_computation.2 | async-start | bytes 1835008 | tf_op jit(solution)/shard_map/all_to_all | solution.py:10
  236.2 8.0 %copy-start = (bf16[1,64,3584]{2,1,0:T(8,128)(2,1)S(1)}, bf16[1,64,3584]{2,1,0:T(8,128)(2,1)}, u32[]{:S(2)}) copy-start(bf16[1,64,3584]{2,1,0:T(8,128)(2,1)} %param.6) | copy-start | bytes 1376260
Sparse Core Ops, SparseCore 0:
  11.3 95.4 all-gather.4
  110.1 87.3 all-gather.6
where the time goes:
time: 264 us; the launch traced here: 263 us
  waiting for transfers between devices  85.8 us (32%)
  blocking collectives  61.8 us (23%)
  local copies, waits for them, and re-layouts  42.5 us (16%)
  matrix products  23.6 us (9%)
  starting transfers between devices  17.8 us (7%)
  other arithmetic  16.4 us (6%)
  between operations  15 us (6%)
    all_gather x1, waiting for transfers between devices, shards(): lax.all_gather(question_embedding_table, 'blk', axis=0, tiled=True)  42.7 us
    all_to_all x1, waiting for transfers between devices, shards(): lax.all_to_all(fetched, 'dp', split_axis=0, concat_axis=0, tiled=True)  38.1 us
    unnamed x1, blocking collectives  32.8 us
    all_to_all x1, blocking collectives, shards(): lax.all_to_all(requests, 'dp', split_axis=0, concat_axis=0, tiled=True)  29 us
    all_to_all x1, starting transfers between devices, return_terms(): lax.all_to_all(outgoing, 'dp', split_axis=0, concat_axis=0, tiled=True)  13.8 us
    scatter x2, local copies, waits for them, and re-layouts, shards(): outgoing = jnp.zeros((shard_count, capacity, width), jnp.bfloat16).at[own...  10.5 us
    convert_element_type x1, other arithmetic, shards(): widened = segment.astype(jnp.float32)  10.4 us
    dot_general x1, matrix products, shards(): lax.dot_general(normalized_exponential_shares, segment, (((0,), (0,)), ((...  9.01 us
  transfers between devices with their start and end apart: 4, of which 3 were waited for; matrix products, arithmetic and copies ran while one was open for 30% of the time, Pallas kernels for 0%

commit v1 on v0

v1 whole, which is shorter than its diff:
```python
import functools

import jax
import jax.numpy as jnp
from jax import lax
from jax.experimental import pallas as pl
from jax.experimental.pallas import tpu as pltpu
from jax.sharding import PartitionSpec as P

SCALE = 50.0
MESH = pl.DeviceIdType.MESH
N_X, N_Z, N_DP, CAP = 4, 16, 32, 3
LANES = 128
P_ROWS, Q_ROWS = 96, 80
CHUNK = 512
BF, F32 = jnp.bfloat16, jnp.float32

S_Q, S_P, S_ST, S_DQ, S_DP, S_REQ, S_PF, S_QP, S_HW = 0, 4, 8, 12, 16, 20, 52, 84, 116
N_SEM = 148


def iota(shape, dim):
    return lax.broadcasted_iota(jnp.int32, shape, dim)


def dot(a, b, contract=((1,), (0,))):
    return lax.dot_general(a, b, (contract, ((), ())), preferred_element_type=F32)


def split(a):
    high = a.astype(BF)
    return high, (a - high.astype(F32)).astype(BF)


def kernel(
    meta, q, p, loss_out, qd_out, pg_out,
    qg, pc, pscr, qscr, pbuf, qbuf, precv, qrecv, pn, qn, neg,
    req, req_in, hw, hw_in, stats, stats_in,
    dqf, dqs, dq_in, dpf, dps, dpc_in, dpy, dpy_in,
    send, recv, local,
):
    rows, width = q.shape
    wide = N_X * rows
    chunks = width // CHUNK
    blk, dp = lax.axis_index("blk"), lax.axis_index("dp")
    core, x, yh = lax.rem(blk, 2), lax.rem(blk // 2, N_X), blk // (2 * N_X)
    z, yl = lax.rem(dp, N_Z), dp // N_Z
    other_core, other_yh = blk + 1 - 2 * core, blk + 2 * N_X - 4 * N_X * yh
    mine, across = yh * 2 + core, (1 - yh) * 2 + core

    def x_peer(d):
        to = lax.rem(x + d, N_X)
        return to, (yh * N_X + to) * 2 + core

    def dp_peer(t):
        dy = lax.rem(t, 2)
        k = t // 2
        half = (k + 1) // 2
        odd = lax.rem(k, 2)
        dz = lax.rem(N_Z // 2 + half - 2 * half * odd + N_Z, N_Z)
        return (
            lax.rem(yl + dy, 2) * N_Z + lax.rem(z + dz, N_Z),
            lax.rem(yl + dy, 2) * N_Z + lax.rem(z - dz + N_Z, N_Z),
        )

    self_t = 2 * (N_Z - 1)

    def each_partner(act):
        def step(t, carry):
            act(t)
            return carry

        lax.fori_loop(0, self_t, step, 0)
        act(self_t + 1)

    def remote(src, dst, slot, **to):
        return pltpu.make_async_remote_copy(
            src_ref=src,
            dst_ref=dst,
            send_sem=send.at[slot],
            recv_sem=recv.at[slot],
            device_id={"blk": blk, "dp": dp, **to},
            device_id_type=MESH,
        )

    barrier = pltpu.get_barrier_semaphore()

    def greet(**to):
        pl.semaphore_signal(barrier, inc=1, device_id={"blk": blk, "dp": dp, **to}, device_id_type=MESH)

    for d in range(1, N_X):
        greet(blk=x_peer(d)[1])
    greet(blk=other_core)
    greet(blk=other_yh)
    each_partner(lambda t: greet(dp=dp_peer(t)[0]))

    keep_q = pltpu.make_async_copy(q, qg.at[x], local.at[0])
    keep_p = pltpu.make_async_copy(p, pc.at[mine], local.at[1])
    keep_q.start()
    keep_p.start()

    owner_row = meta[1:2, :rows].astype(F32)
    slot_row = meta[2:3, :rows].astype(F32)
    r0, r1 = iota((rows, rows), 0), iota((rows, rows), 1)
    eye = r0 == r1

    def column(row):
        return jnp.sum(jnp.where(eye, row, 0.0), axis=1, keepdims=True)

    owner_col = column(owner_row)
    same = jnp.where(owner_col == owner_row, 1.0, 0.0)
    rank_col = jnp.sum(jnp.where(r1 < r0, same, 0.0), axis=1, keepdims=True)
    rank_row = jnp.sum(jnp.where(r0 < r1, same, 0.0), axis=0, keepdims=True)
    key_row = rank_row * N_DP + owner_row
    key_col = rank_col * N_DP + owner_col
    slots = N_DP * CAP
    by_slot = key_row == iota((slots, rows), 0).astype(F32)
    by_row = key_col == iota((rows, slots), 1).astype(F32)
    lane = iota((N_DP, LANES), 1)

    def table(row):
        out = jnp.zeros((N_DP, LANES), F32)
        for c in range(CAP):
            picked = jnp.where(by_slot[c * N_DP : (c + 1) * N_DP], row, 0.0)
            out = jnp.where(lane == c, jnp.sum(picked, axis=1, keepdims=True), out)
        return out

    every_8th = pl.ds(0, N_DP, stride=8)
    stats[...] = jnp.zeros_like(stats)
    req[...] = jnp.zeros_like(req)
    hw[...] = jnp.zeros_like(hw)
    req[every_8th, :] = table(slot_row + 1.0)
    pscr[...] = jnp.zeros_like(pscr)

    pl.semaphore_wait(barrier, N_X + 1 + N_DP - 1)

    def table_copy(src, dst, base, t):
        to, _ = dp_peer(t)
        return remote(
            src.at[pl.ds(pl.multiple_of(to * 8, 8), 8)],
            dst.at[pl.ds(pl.multiple_of(dp * 8, 8), 8)],
            base + t,
            dp=to,
        )

    def rows_copy(src, dst, base, t):
        to, _ = dp_peer(t)
        return remote(src.at[to], dst.at[dp], base + t, dp=to)

    request = functools.partial(table_copy, req, req_in, S_REQ)
    weight = functools.partial(table_copy, hw, hw_in, S_HW)
    fetch = functools.partial(rows_copy, pbuf, precv, S_PF)
    push = functools.partial(rows_copy, qbuf, qrecv, S_QP)

    each_partner(lambda t: request(t).start())

    q_copies = [remote(q, qg.at[x], S_Q + d, blk=x_peer(d)[1]) for d in range(1, N_X)]
    p_core = remote(p, pc.at[mine], S_P, blk=other_core)
    p_across = remote(p, pc.at[mine], S_P + 1, blk=other_yh)
    p_across.start()
    for copy in q_copies:
        copy.start()
    p_core.start()

    def lay_out(onehot, source, place):
        for n in range(chunks):
            packed = dot(onehot, source[:, n * CHUNK : (n + 1) * CHUNK])
            for c in range(CAP):
                for k in range(CHUNK // LANES):
                    ref, at, stride = place(c * (width // LANES) + n * (CHUNK // LANES) + k)
                    ref[pl.ds(at, N_DP, stride=stride), :] = packed[
                        c * N_DP : (c + 1) * N_DP, k * LANES : (k + 1) * LANES
                    ]

    def place_q(i):
        return (qscr, i, Q_ROWS) if i < Q_ROWS else (pscr, 84 + i - Q_ROWS, P_ROWS)

    def place_p(i):
        return (pscr, i, P_ROWS)

    lay_out(jnp.where(by_slot, 1.0, 0.0).astype(BF), q, place_q)

    def round_q(a, carry):
        qbuf[a] = qscr[pl.ds(pl.multiple_of(a * Q_ROWS, 16), Q_ROWS), :].astype(BF)
        return carry

    lax.fori_loop(0, N_DP, round_q, 0)

    each_partner(lambda t: request(t).wait_recv())
    req_in[pl.ds(pl.multiple_of(dp * 8, 8), 8), :] = req[pl.ds(pl.multiple_of(dp * 8, 8), 8), :]
    asked = req_in[every_8th, :] - 1.0

    def by_asked(values):
        row_of = iota((N_DP, rows), 1).astype(F32)
        return jnp.concatenate(
            [jnp.where(asked[:, c : c + 1] == row_of, values[:, c : c + 1], 0.0) for c in range(CAP)],
            axis=0,
        )

    lay_out(by_asked(jnp.ones((N_DP, LANES), F32)).astype(BF), p, place_p)

    def round_p(a, carry):
        pbuf[a] = pscr[pl.ds(pl.multiple_of(a * P_ROWS, 16), P_ROWS), :].astype(BF)
        return carry

    lax.fori_loop(0, N_DP, round_p, 0)
    each_partner(lambda t: fetch(t).start())
    each_partner(lambda t: push(t).start())
    precv[dp] = pbuf[dp]
    qrecv[dp] = qbuf[dp]

    p_across.wait_recv()
    p_pass = remote(pc.at[across], pc.at[across], S_P + 2, blk=other_core)
    p_pass.start()
    keep_q.wait()
    keep_p.wait()
    for copy in q_copies:
        copy.wait_recv()
    p_core.wait_recv()
    p_pass.wait_recv()

    def columns(n):
        return pl.ds(pl.multiple_of(n * CHUNK, CHUNK), CHUNK)

    def add_scores(n, total):
        return total + dot(
            pc[:, :, columns(n)].reshape(wide, CHUNK),
            qg[:, :, columns(n)].reshape(wide, CHUNK),
            ((1,), (1,)),
        )

    scores = SCALE * lax.fori_loop(0, chunks, add_scores, jnp.zeros((wide, wide), F32))
    row = iota((wide, 1), 0)
    index = ((row // (2 * rows)) * N_X + x) * 2 * rows + lax.rem(row, 2 * rows)
    paired = jnp.where(index == meta[0:1, :], 1.0, 0.0)
    peak = jnp.max(scores, axis=0, keepdims=True)
    total = jnp.sum(jnp.exp(scores - peak), axis=0, keepdims=True)
    picked = jnp.sum(paired * scores, axis=0, keepdims=True)

    each_partner(lambda t: fetch(t).wait_recv())

    def widen_p(a, carry):
        pscr[pl.ds(pl.multiple_of(a * P_ROWS, 8), P_ROWS), :] = precv[a].astype(F32)
        return carry

    lax.fori_loop(0, N_DP, widen_p, 0)

    def gather_rows(out, place):
        for n in range(width // LANES):
            for c in range(CAP):
                ref, at, stride = place(c * (width // LANES) + n)
                out[c * N_DP : (c + 1) * N_DP, n * LANES : (n + 1) * LANES] = ref[
                    pl.ds(at, N_DP, stride=stride), :
                ].astype(BF)

    gather_rows(pn, place_p)
    pick = jnp.where(by_row, 1.0, 0.0).astype(BF)

    def take_negatives(n, total):
        rows_of = dot(pick, pn[:, columns(n)])
        neg[:, columns(n)] = rows_of.astype(BF)
        return total + rows_of * q[:, columns(n)].astype(F32)

    products = lax.fori_loop(0, chunks, take_negatives, jnp.zeros((rows, CHUNK), F32))
    hard_col = SCALE * jnp.sum(products, axis=1, keepdims=True)
    shifted = iota((rows, wide), 1) == iota((rows, wide), 0) + x * rows
    hard_wide = jnp.sum(jnp.where(shifted, hard_col, 0.0), axis=0, keepdims=True)
    own = iota((1, wide), 1) // rows == x
    peak_own = jnp.where(own, jnp.maximum(peak, hard_wide), peak)
    total = total * jnp.exp(peak - peak_own) + jnp.where(own, jnp.exp(hard_wide - peak_own), 0.0)
    stats[0:1, :] = peak_own
    stats[1:2, :] = total
    stats[2:3, :] = picked
    st_copies = [remote(stats, stats_in.at[x], S_ST + d, blk=x_peer(d)[1]) for d in range(1, N_X)]
    for copy in st_copies:
        copy.start()
    stats_in[x] = stats[...]
    for copy in st_copies:
        copy.wait_recv()
    peaks = [stats_in[i, 0:1, :] for i in range(N_X)]
    top = functools.reduce(jnp.maximum, peaks)
    whole = sum(stats_in[i, 1:2, :] * jnp.exp(peaks[i] - top) for i in range(N_X))
    lse = top + jnp.log(whole)
    loss_wide = lse - sum(stats_in[i, 2:3, :] for i in range(N_X))

    def own_column(wide_row):
        return jnp.sum(jnp.where(shifted, wide_row, 0.0), axis=1, keepdims=True)

    loss_out[...] = jnp.sum(jnp.where(eye, own_column(loss_wide), 0.0), axis=0, keepdims=True)
    hard_weight_col = jnp.exp(hard_col - own_column(lse))
    hard_weight_row = jnp.sum(jnp.where(eye, hard_weight_col, 0.0), axis=0, keepdims=True)
    hw[every_8th, :] = table(hard_weight_row)
    each_partner(lambda t: weight(t).start())

    weights = jnp.exp(scores - lse)
    high, low = split((weights - paired).T)

    def query_terms(n, carry):
        part = pc[:, :, columns(n)].reshape(wide, CHUNK)
        out = (SCALE * (dot(high, part) + dot(low, part))).reshape(N_X, rows, CHUNK)
        dqf[:, :, columns(n)] = out
        dqs[:, :, columns(n)] = out.astype(BF)
        return carry

    lax.fori_loop(0, chunks, query_terms, 0)
    dq_copies = [
        remote(dqs.at[x_peer(d)[0]], dq_in.at[d], S_DQ + d, blk=x_peer(d)[1]) for d in range(1, N_X)
    ]
    for copy in dq_copies:
        copy.start()

    probs, pairs = weights.astype(BF), paired.astype(BF)

    def passage_terms(n, carry):
        part = qg[:, :, columns(n)].reshape(wide, CHUNK)
        out = (SCALE * (dot(probs, part) - dot(pairs, part))).reshape(N_X, rows, CHUNK)
        dpf[:, :, columns(n)] = out
        dps[:, :, columns(n)] = out.astype(BF)
        return carry

    lax.fori_loop(0, chunks, passage_terms, 0)
    dp_across = remote(dps.at[(1 - yh) * 2 + 1 - core], dpc_in.at[1], S_DP, blk=other_core)
    dp_here = remote(dps.at[yh * 2 + 1 - core], dpc_in.at[0], S_DP + 1, blk=other_core)
    dp_across.start()
    dp_here.start()
    dp_across.wait_recv()

    def sum_across(n, carry):
        dpy[:, columns(n)] = (dpf[across, :, columns(n)] + dpc_in[1, :, columns(n)].astype(F32)).astype(BF)
        return carry

    lax.fori_loop(0, chunks, sum_across, 0)
    dp_y = remote(dpy, dpy_in, S_DP + 2, blk=other_yh)
    dp_y.start()

    for copy in dq_copies:
        copy.wait_recv()

    def query_sum(n, carry):
        out = dqf[x, :, columns(n)] + SCALE * hard_weight_col * neg[:, columns(n)].astype(F32)
        for d in range(1, N_X):
            out = out + dq_in[d, :, columns(n)].astype(F32)
        qd_out[:, columns(n)] = out.astype(BF)
        return carry

    lax.fori_loop(0, chunks, query_sum, 0)

    each_partner(lambda t: weight(t).wait_recv())
    hw_in[pl.ds(pl.multiple_of(dp * 8, 8), 8), :] = hw[pl.ds(pl.multiple_of(dp * 8, 8), 8), :]
    hard_high, hard_low = split(by_asked(hw_in[every_8th, :]).T)
    each_partner(lambda t: push(t).wait_recv())

    def widen_q(a, carry):
        qscr[pl.ds(pl.multiple_of(a * Q_ROWS, 8), Q_ROWS), :] = qrecv[a].astype(F32)
        return carry

    lax.fori_loop(0, N_DP, widen_q, 0)
    gather_rows(qn, place_q)
    dp_here.wait_recv()
    dp_y.wait_recv()

    def passage_sum(n, carry):
        terms = qn[:, columns(n)]
        out = dpf[mine, :, columns(n)] + SCALE * (dot(hard_high, terms) + dot(hard_low, terms))
        out = out + dpc_in[0, :, columns(n)].astype(F32) + dpy_in[:, columns(n)].astype(F32)
        pg_out[:, columns(n)] = out.astype(BF)
        return carry

    lax.fori_loop(0, chunks, passage_sum, 0)

    for copy in (*q_copies, p_core, p_across, p_pass, *st_copies, *dq_copies, dp_across, dp_here, dp_y):
        copy.wait_send()

    def sent(t):
        request(t).wait_send()
        fetch(t).wait_send()
        push(t).wait_send()
        weight(t).wait_send()

    each_partner(sent)


def shards(queries, passages, positive, hard_owner, hard_slot):
    q, p = queries[0], passages[0]
    rows, width = q.shape
    wide = N_X * rows
    blk = lax.axis_index("blk")
    places = positive.reshape(2, N_X, 2, rows)
    places = lax.dynamic_index_in_dim(places, blk // (2 * N_X), 0, keepdims=False)
    places = lax.dynamic_index_in_dim(places, lax.rem(blk, 2), 1, keepdims=False)
    pad = ((0, 0), (0, wide - rows))
    meta = jnp.concatenate(
        [
            places.reshape(1, wide),
            jnp.pad(hard_owner.reshape(1, rows), pad),
            jnp.pad(hard_slot.reshape(1, rows), pad),
        ],
        axis=0,
    )
    vmem = pl.BlockSpec(memory_space=pltpu.VMEM)
    block = (rows, width)
    loss, qd, pg = pl.pallas_call(
        kernel,
        out_shape=(
            jax.ShapeDtypeStruct((1, rows), F32),
            jax.ShapeDtypeStruct(block, BF),
            jax.ShapeDtypeStruct(block, BF),
        ),
        in_specs=[vmem] * 3,
        out_specs=[vmem] * 3,
        scratch_shapes=[
            pltpu.VMEM((N_X, *block), BF),
            pltpu.VMEM((N_X, *block), BF),
            pltpu.VMEM((N_DP * P_ROWS, LANES), F32),
            pltpu.VMEM((N_DP * Q_ROWS, LANES), F32),
            pltpu.VMEM((N_DP, P_ROWS, LANES), BF),
            pltpu.VMEM((N_DP, Q_ROWS, LANES), BF),
            pltpu.VMEM((N_DP, P_ROWS, LANES), BF),
            pltpu.VMEM((N_DP, Q_ROWS, LANES), BF),
            pltpu.VMEM((N_DP * CAP, width), BF),
            pltpu.VMEM((N_DP * CAP, width), BF),
            pltpu.VMEM(block, BF),
            pltpu.VMEM((N_DP * 8, LANES), F32),
            pltpu.VMEM((N_DP * 8, LANES), F32),
            pltpu.VMEM((N_DP * 8, LANES), F32),
            pltpu.VMEM((N_DP * 8, LANES), F32),
            pltpu.VMEM((8, wide), F32),
            pltpu.VMEM((N_X, 8, wide), F32),
            pltpu.VMEM((N_X, *block), F32),
            pltpu.VMEM((N_X, *block), BF),
            pltpu.VMEM((N_X, *block), BF),
            pltpu.VMEM((N_X, *block), F32),
            pltpu.VMEM((N_X, *block), BF),
            pltpu.VMEM((2, *block), BF),
            pltpu.VMEM(block, BF),
            pltpu.VMEM(block, BF),
            pltpu.SemaphoreType.DMA((N_SEM,)),
            pltpu.SemaphoreType.DMA((N_SEM,)),
            pltpu.SemaphoreType.DMA((2,)),
        ],
        compiler_params=pltpu.CompilerParams(
            collective_id=0, has_side_effects=True, vmem_limit_bytes=56 * 2**20
        ),
        cost_estimate=pl.CostEstimate(flops=3 * 10**9, bytes_accessed=2 * 10**6, transcendentals=2 * 10**5),
    )(meta, q, p)
    return loss, qd[None], pg[None]


def solution(mesh):
    placed = (
        P("dp", "blk", None),
        P("dp", "blk", None),
        P("dp", None),
        P("dp", "blk", None),
        P("dp", "blk", None),
    )
    return jax.shard_map(
        shards,
        mesh=mesh,
        in_specs=placed,
        out_specs=(P("dp", "blk"), P("dp", "blk", None), P("dp", "blk", None)),
        check_vma=False,
    )
```

time: 264 us -> 111 us (0.42)
  Pallas kernels: 0 us -> 103 us
  waiting for transfers between devices: 85.8 us -> 0 us
  blocking collectives: 61.8 us -> 0 us
  local copies, waits for them, and re-layouts: 42.5 us -> 5.23 us
  matrix products: 23.6 us -> 0 us
  starting transfers between devices: 17.8 us -> 0 us
  other arithmetic: 16.4 us -> 1.26 us
  between operations: 15 us -> 0.71 us
    pallas_call x0 -> x1, Pallas kernels: none -> 103 us  [shards(): pl.pallas_call(kernel, out_shape=(jax.ShapeDtypeStruct((1, rows), F32), j...]
    all_gather x2 -> x0, waiting for transfers between devices: 46.3 us -> none  [the longest x1 42.7 us: shards(): lax.all_gather(question_embedding_table, 'blk', axis=0, tiled=True)]
    all_to_all x2 -> x0, waiting for transfers between devices: 38.1 us -> none  [the longest x1 38.1 us: shards(): lax.all_to_all(fetched, 'dp', split_axis=0, concat_axis=0, tiled=True)]
    unnamed x1 -> x0, blocking collectives: 32.8 us -> none
    all_to_all x1 -> x0, blocking collectives: 29 us -> none  [shards(): lax.all_to_all(requests, 'dp', split_axis=0, concat_axis=0, tiled=True)]
    dot_general x4 -> x0, matrix products: 23.6 us -> none  [the longest x1 9.01 us: shards(): lax.dot_general(normalized_exponential_shares, segment, (((0,), (0,)), ((...]
    scatter x4 -> x0, local copies, waits for them, and re-layouts: 20.5 us -> none  [the longest x2 10.5 us: shards(): outgoing = jnp.zeros((shard_count, capacity, width), jnp.bfloat16).at[own...]
    gather x6 -> x0, local copies, waits for them, and re-layouts: 17.9 us -> none  [the longest x1 6.46 us: shards(): paired_target_logits = jnp.where(inside[:, None], widened[clipped], 0.0)]
  transfers between devices with their start and end apart: 4 -> 0, of which waited for: 3 -> 0; matrix products, arithmetic and copies ran while one was open for 30% -> 0% of each run, Pallas kernels for 0% -> 0%
where the time goes in v1:
time: 111 us; the launch traced here: 110 us
  Pallas kernels  103 us (93%)
  local copies, waits for them, and re-layouts  5.23 us (5%)
  other arithmetic  1.26 us (1%)
    pallas_call x1, Pallas kernels, shards(): pl.pallas_call(kernel, out_shape=(jax.ShapeDtypeStruct((1, rows), F32), j...  103 us
    unnamed x14, local copies, waits for them, and re-layouts  5.06 us

profile of v1, /device:TPU:1, one launch (start us, length us, event | category | flops | bytes accessed | tf_op | source)
XLA Modules:
  0.0 110.4 jit_solution(9354199587319732803)
XLA Ops:
  0.7 0.0 copy-start.1
  0.7 0.5 broadcast.9
  1.2 0.2 copy-done.1
  1.3 0.7 reduce.3
  2.0 0.1 reshape.21
  2.1 0.0 copy-start.2
  2.1 0.0 copy-start.3
  2.1 0.1 reshape.22
  2.2 0.6 copy-done.2
  2.8 0.0 copy-done.3
  2.8 0.6 pad_add_fusion.meta
  3.4 103.2 %shard_map.76 = (f32[1,64]{1,0:T(1,128)}, bf16[64,3584]{1,0:T(8,128)(2,1)}, bf16[64,3584]{1,0:T(8,128)(2,1)}) custom-call(s32[3,256]{1,0:T(4,128)} %pad_add_fusion.meta, bf16[64,3584]{1,0:T(8,128)(2,1)} %bitcast.14, bf16[64,3584]{1,0:T(8,128)(2,1)} %bitcast.15), custom_call_target="tpu_custom_call" | custom-call | flops 3000000000 | bytes 2000000 | tf_op jit(solution)/shard_map/pallas_call | solution.py:402
  106.6 0.0 copy-start.4
  106.6 0.7 copy-done.4
  107.3 0.5 copy.13
  107.8 0.0 copy-start
  107.8 1.9 %copy.14 = bf16[1,64,3584]{2,1,0:T(8,128)(2,1)} copy(bf16[1,64,3584]{2,1,0:T(8,128)(2,1)} %bitcast.10) | data formatting | bytes 917504
  109.7 0.0 copy-done
  109.7 0.8 copy.15
  (1 shorter events, 0.0 us)
Async XLA Ops:
  0.7 0.7 copy-start.1
  2.1 0.7 copy-start.2
  2.1 0.7 copy-start.3
  106.6 0.7 copy-start.4
  107.8 1.9 %copy-start = (bf16[64,3584]{1,0:T(8,128)(2,1)S(1)}, bf16[64,3584]{1,0:T(8,128)(2,1)}, u32[]{:S(2)}) copy-start(bf16[64,3584]{1,0:T(8,128)(2,1)} %get-tuple-element.8) | copy-start | bytes 1376260

commit v2 on v1

v2 whole, which is shorter than its diff:
```python
import functools

import jax
import jax.numpy as jnp
from jax import lax
from jax.experimental import pallas as pl
from jax.experimental.pallas import tpu as pltpu
from jax.sharding import PartitionSpec as P

SCALE = 50.0
MESH = pl.DeviceIdType.MESH
N_X, N_Z, N_DP, CAP = 4, 16, 32, 3
LANES = 128
P_ROWS, Q_ROWS = 96, 80
CHUNK = 512
BF, F32 = jnp.bfloat16, jnp.float32

S_Q, S_P, S_ST, S_DP, S_AL, S_DQ, S_PP, S_REQ, S_PF, S_QP, S_HW = 0, 4, 8, 12, 16, 20, 26, 32, 64, 96, 128
N_SEM = 160
EARLY = 4


def iota(shape, dim):
    return lax.broadcasted_iota(jnp.int32, shape, dim)


def dot(a, b, contract=((1,), (0,))):
    return lax.dot_general(a, b, (contract, ((), ())), preferred_element_type=F32)


def split(a):
    high = a.astype(BF)
    return high, (a - high.astype(F32)).astype(BF)


def kernel(
    positive, owner, slot, q_in, p_in, loss_out, qd_out, pg_out,
    qg, pc, pscr, qscr, pbuf, qbuf, precv, qrecv, pn, qn, neg,
    req, req_in, hw, hw_in, stats, stats_in, alphas, alphas_in,
    tf, ts, t_in, t_pass, t_sum, pps, pp_in, pp_pass, pp_sum, dpf, dps, dpc_in, dpy, dpy_in,
    send, recv, local,
):
    rows, width = q_in.shape
    wide = N_X * rows
    chunks = width // CHUNK
    blk, dp = lax.axis_index("blk"), lax.axis_index("dp")
    core, x, yh = lax.rem(blk, 2), lax.rem(blk // 2, N_X), blk // (2 * N_X)
    z, yl = lax.rem(dp, N_Z), dp // N_Z
    other_core, other_yh = blk + 1 - 2 * core, blk + 2 * N_X - 4 * N_X * yh
    mine, across = yh * 2 + core, (1 - yh) * 2 + core

    def x_peer(d):
        to = lax.rem(x + d, N_X)
        return to, (yh * N_X + to) * 2 + core

    right_x, right = x_peer(1)
    left_x, left = x_peer(N_X - 1)
    opposite = lax.rem(x + 2, N_X)
    half = width // 2
    low_half, high_half = pl.ds(0, half), pl.ds(half, half)

    def dp_peer(t):
        dy = lax.rem(t, 2)
        k = t // 2
        half = (k + 1) // 2
        odd = lax.rem(k, 2)
        dz = lax.rem(N_Z // 2 + half - 2 * half * odd + N_Z, N_Z)
        y = lax.rem(yl + dy, 2) * N_Z
        return y + lax.rem(z + dz, N_Z), y + lax.rem(z - dz + N_Z, N_Z)

    self_t = 2 * (N_Z - 1)

    def each_partner(act, first=0):
        def step(t, carry):
            act(t)
            return carry

        lax.fori_loop(first, self_t, step, 0)
        act(self_t + 1)

    def remote(src, dst, sem, **to):
        return pltpu.make_async_remote_copy(
            src_ref=src,
            dst_ref=dst,
            send_sem=send.at[sem],
            recv_sem=recv.at[sem],
            device_id={"blk": blk, "dp": dp, **to},
            device_id_type=MESH,
        )

    barrier = pltpu.get_barrier_semaphore()

    def greet(**to):
        pl.semaphore_signal(barrier, inc=1, device_id={"blk": blk, "dp": dp, **to}, device_id_type=MESH)

    each_partner(lambda t: greet(dp=dp_peer(t)[0]))
    for d in range(1, N_X):
        greet(blk=x_peer(d)[1])
    greet(blk=other_core)
    greet(blk=other_yh)

    keep_q = pltpu.make_async_copy(q_in, qg.at[x], local.at[0])
    keep_p = pltpu.make_async_copy(p_in, pc.at[mine], local.at[1])
    keep_q.start()
    keep_p.start()

    owner_row = owner[...].astype(F32)
    slot_row = slot[...].astype(F32)
    r0, r1 = iota((rows, rows), 0), iota((rows, rows), 1)
    eye = r0 == r1

    def column(row):
        return jnp.sum(jnp.where(eye, row, 0.0), axis=1, keepdims=True)

    owner_col = column(owner_row)
    same = jnp.where(owner_col == owner_row, 1.0, 0.0)
    rank_col = jnp.sum(jnp.where(r1 < r0, same, 0.0), axis=1, keepdims=True)
    rank_row = jnp.sum(jnp.where(r0 < r1, same, 0.0), axis=0, keepdims=True)
    key_row = rank_row * N_DP + owner_row
    key_col = rank_col * N_DP + owner_col
    slots = N_DP * CAP
    by_slot = key_row == iota((slots, rows), 0).astype(F32)
    by_row = key_col == iota((rows, slots), 1).astype(F32)
    lane = iota((N_DP, LANES), 1)

    def table(row):
        out = jnp.zeros((N_DP, LANES), F32)
        for c in range(CAP):
            picked = jnp.where(by_slot[c * N_DP : (c + 1) * N_DP], row, 0.0)
            out = jnp.where(lane == c, jnp.sum(picked, axis=1, keepdims=True), out)
        return out

    every_8th = pl.ds(0, N_DP, stride=8)
    req[...] = jnp.zeros_like(req)
    req[every_8th, :] = table(slot_row + 1.0)
    hw[...] = jnp.zeros_like(hw)
    stats[...] = jnp.zeros_like(stats)
    alphas[...] = jnp.zeros_like(alphas)
    pscr[...] = jnp.zeros_like(pscr)

    def columns(n):
        return pl.ds(pl.multiple_of(n * CHUNK, CHUNK), CHUNK)

    def lay_out(onehot, ref_of, place):
        for n in range(chunks):
            packed = dot(onehot, ref_of(n))
            for c in range(CAP):
                for k in range(CHUNK // LANES):
                    ref, at, stride = place(c * (width // LANES) + n * (CHUNK // LANES) + k)
                    ref[pl.ds(at, N_DP, stride=stride), :] = packed[
                        c * N_DP : (c + 1) * N_DP, k * LANES : (k + 1) * LANES
                    ]

    def place_q(i):
        return (qscr, i, Q_ROWS) if i < Q_ROWS else (pscr, 84 + i - Q_ROWS, P_ROWS)

    def place_p(i):
        return (pscr, i, P_ROWS)

    keep_q.wait()
    lay_out(
        jnp.where(by_slot, 1.0, 0.0).astype(BF),
        lambda n: qg[x, :, n * CHUNK : (n + 1) * CHUNK],
        place_q,
    )

    def round_q(a, carry):
        qbuf[a] = qscr[pl.ds(pl.multiple_of(a * Q_ROWS, 16), Q_ROWS), :].astype(BF)
        return carry

    lax.fori_loop(0, N_DP, round_q, 0)
    keep_p.wait()
    pl.semaphore_wait(barrier, N_X + 1 + N_DP - 1)

    def table_copy(src, dst, base, t):
        to, _ = dp_peer(t)
        return remote(
            src.at[pl.ds(pl.multiple_of(to * 8, 8), 8)],
            dst.at[pl.ds(pl.multiple_of(dp * 8, 8), 8)],
            base + t,
            dp=to,
        )

    def rows_copy(src, dst, base, t):
        to, _ = dp_peer(t)
        return remote(src.at[to], dst.at[dp], base + t, dp=to)

    request = functools.partial(table_copy, req, req_in, S_REQ)
    weight = functools.partial(table_copy, hw, hw_in, S_HW)
    fetch = functools.partial(rows_copy, pbuf, precv, S_PF)
    push = functools.partial(rows_copy, qbuf, qrecv, S_QP)

    each_partner(lambda t: request(t).start())
    for t in range(EARLY):
        push(t).start()

    q_right = remote(qg.at[x], qg.at[x], S_Q, blk=right)
    q_left = remote(qg.at[x], qg.at[x], S_Q + 1, blk=left)
    p_core = remote(pc.at[mine], pc.at[mine], S_P, blk=other_core)
    p_across = remote(pc.at[mine], pc.at[mine], S_P + 1, blk=other_yh)
    p_across.start()
    q_right.start()
    q_left.start()
    p_core.start()

    each_partner(lambda t: request(t).wait_recv())
    req_in[pl.ds(pl.multiple_of(dp * 8, 8), 8), :] = req[pl.ds(pl.multiple_of(dp * 8, 8), 8), :]
    asked = req_in[every_8th, :] - 1.0

    def by_asked(values):
        row_of = iota((N_DP, rows), 1).astype(F32)
        return jnp.concatenate(
            [jnp.where(asked[:, c : c + 1] == row_of, values[:, c : c + 1], 0.0) for c in range(CAP)],
            axis=0,
        )

    lay_out(
        by_asked(jnp.ones((N_DP, LANES), F32)).astype(BF),
        lambda n: pc[mine, :, n * CHUNK : (n + 1) * CHUNK],
        place_p,
    )

    def round_p(a, carry):
        pbuf[a] = pscr[pl.ds(pl.multiple_of(a * P_ROWS, 16), P_ROWS), :].astype(BF)
        return carry

    lax.fori_loop(0, N_DP, round_p, 0)
    each_partner(lambda t: fetch(t).start())
    each_partner(lambda t: push(t).start(), EARLY)
    precv[dp] = pbuf[dp]
    qrecv[dp] = qbuf[dp]

    p_across.wait_recv()
    p_pass = remote(pc.at[across], pc.at[across], S_P + 2, blk=other_core)
    p_pass.start()
    q_right.wait_recv()
    q_on = remote(qg.at[left_x, :, low_half], qg.at[left_x, :, low_half], S_Q + 2, blk=right)
    q_on.start()
    q_left.wait_recv()
    q_back = remote(qg.at[right_x, :, high_half], qg.at[right_x, :, high_half], S_Q + 3, blk=left)
    q_back.start()

    lanes = iota((8, LANES), 1)
    halves = []
    for i in range(N_X):
        chunk = positive[0:1, pl.ds(pl.multiple_of((yh * N_X + i) * LANES, LANES), LANES)]
        chunk = jnp.broadcast_to(chunk, (8, LANES))
        halves.append(jnp.where(core == i % 2, chunk, pltpu.roll(chunk, rows, 1)))
    positive_wide = jnp.concatenate(
        [jnp.where(lanes < rows, halves[i], halves[i + 1]) for i in range(0, N_X, 2)], axis=1
    )[0:1, :]
    row = iota((wide, 1), 0)
    index = ((row // (2 * rows)) * N_X + x) * 2 * rows + lax.rem(row, 2 * rows)
    paired = jnp.where(index == positive_wide, 1.0, 0.0)

    p_core.wait_recv()
    p_pass.wait_recv()

    pairs = paired.astype(BF)
    pairs_by_query = paired.T.astype(BF)

    def ring_first(blocks, passing, into, base):
        copies = [
            remote(blocks.at[opposite, :, low_half], passing.at[0], base, blk=right),
            remote(blocks.at[opposite, :, high_half], passing.at[1], base + 1, blk=left),
            remote(blocks.at[right_x, :, high_half], into.at[0, :, high_half], base + 2, blk=right),
            remote(blocks.at[left_x, :, low_half], into.at[1, :, low_half], base + 3, blk=left),
        ]
        for copy in copies:
            copy.start()
        return copies

    def ring_second(copies, blocks, passing, sums, into, base):
        copies[0].wait_recv()
        copies[1].wait_recv()
        size = half // chunks

        def add(n, carry):
            at = pl.ds(pl.multiple_of(n * size, size), size)
            beyond = pl.ds(pl.multiple_of(half + n * size, size), size)
            sums[0, :, at] = (blocks[right_x, :, at].astype(F32) + passing[0, :, at].astype(F32)).astype(BF)
            sums[1, :, at] = (blocks[left_x, :, beyond].astype(F32) + passing[1, :, at].astype(F32)).astype(BF)
            return carry

        lax.fori_loop(0, chunks, add, 0)
        more = [
            remote(sums.at[0], into.at[0, :, low_half], base + 4, blk=right),
            remote(sums.at[1], into.at[1, :, high_half], base + 5, blk=left),
        ]
        for copy in more:
            copy.start()
        return copies + more

    q_on.wait_recv()
    q_back.wait_recv()

    def add_scores(n, total):
        return total + dot(
            pc[:, :, columns(n)].reshape(wide, CHUNK),
            qg[:, :, columns(n)].reshape(wide, CHUNK),
            ((1,), (1,)),
        )

    scores = SCALE * lax.fori_loop(0, chunks, add_scores, jnp.zeros((wide, wide), F32))
    peak = jnp.max(scores, axis=0, keepdims=True)
    stats[0:1, :] = peak
    stats[1:2, :] = jnp.sum(jnp.exp(scores - peak), axis=0, keepdims=True)
    stats[2:3, :] = jnp.sum(paired * scores, axis=0, keepdims=True)
    st_copies = [remote(stats, stats_in.at[x], S_ST + d, blk=x_peer(d)[1]) for d in range(1, N_X)]
    for copy in st_copies:
        copy.start()
    stats_in[x] = stats[...]
    for copy in st_copies:
        copy.wait_recv()
    peaks = [stats_in[i, 0:1, :] for i in range(N_X)]
    top = functools.reduce(jnp.maximum, peaks)
    whole = sum(stats_in[i, 1:2, :] * jnp.exp(peaks[i] - top) for i in range(N_X))
    lse_batch = top + jnp.log(whole)
    picked = sum(stats_in[i, 2:3, :] for i in range(N_X))
    weights = jnp.exp(scores - lse_batch)
    high, low = split((weights - paired).T)

    def query_terms(n, carry):
        part = pc[:, :, columns(n)].reshape(wide, CHUNK)
        out = (dot(high, part) + dot(low, part)).reshape(N_X, rows, CHUNK)
        tf[:, :, columns(n)] = out
        ts[:, :, columns(n)] = out.astype(BF)
        return carry

    lax.fori_loop(0, chunks, query_terms, 0)
    t_copies = ring_first(ts, t_pass, t_in, S_DQ)
    def positives(n, carry):
        out = dot(pairs_by_query, pc[:, :, columns(n)].reshape(wide, CHUNK))
        pps[:, :, columns(n)] = out.reshape(N_X, rows, CHUNK).astype(BF)
        return carry

    lax.fori_loop(0, chunks, positives, 0)

    t_copies = ring_second(t_copies, tf, t_pass, t_sum, t_in, S_DQ)

    def widen_p(t):
        fetch(t).wait_recv()
        widen(pscr, precv, P_ROWS, dp_peer(t)[1])

    def widen(out, source, size, a):
        out[pl.ds(pl.multiple_of(a * size, 8), size), :] = source[a].astype(F32)

    widen(pscr, precv, P_ROWS, dp)
    each_partner(widen_p)

    def gather_rows(out, place):
        for n in range(width // LANES):
            for c in range(CAP):
                ref, at, stride = place(c * (width // LANES) + n)
                out[c * N_DP : (c + 1) * N_DP, n * LANES : (n + 1) * LANES] = ref[
                    pl.ds(at, N_DP, stride=stride), :
                ].astype(BF)

    gather_rows(pn, place_p)
    pick = jnp.where(by_row, 1.0, 0.0).astype(BF)

    def take_negatives(n, total):
        rows_of = dot(pick, pn[:, columns(n)])
        neg[:, columns(n)] = rows_of.astype(BF)
        return total + rows_of * qg[x, :, columns(n)].astype(F32)

    products = lax.fori_loop(0, chunks, take_negatives, jnp.zeros((rows, CHUNK), F32))
    hard_col = SCALE * jnp.sum(products, axis=1, keepdims=True)
    shifted = iota((rows, wide), 1) == iota((rows, wide), 0) + x * rows

    def own_column(wide_row):
        return jnp.sum(jnp.where(shifted, wide_row, 0.0), axis=1, keepdims=True)

    batch_col = own_column(lse_batch)
    top_col = jnp.maximum(batch_col, hard_col)
    lse_col = top_col + jnp.log(jnp.exp(batch_col - top_col) + jnp.exp(hard_col - top_col))
    alpha_col = jnp.exp(batch_col - lse_col)
    hard_weight_col = jnp.exp(hard_col - lse_col)
    alphas[0:1, :] = jnp.sum(jnp.where(shifted, alpha_col, 0.0), axis=0, keepdims=True)
    al_copies = [remote(alphas, alphas_in.at[x], S_AL + d, blk=x_peer(d)[1]) for d in range(1, N_X)]
    for copy in al_copies:
        copy.start()
    pp_copies = ring_first(pps, pp_pass, pp_in, S_PP)
    alphas_in[x] = alphas[...]
    hard_weight_row = jnp.sum(jnp.where(eye, hard_weight_col, 0.0), axis=0, keepdims=True)
    hw[every_8th, :] = table(hard_weight_row)
    each_partner(lambda t: weight(t).start())
    for copy in al_copies:
        copy.wait_recv()
    alpha = sum(alphas_in[i, 0:1, :] for i in range(N_X))
    probs = (weights * alpha).astype(BF)

    def passage_terms(n, carry):
        part = qg[:, :, columns(n)].reshape(wide, CHUNK)
        out = (SCALE * (dot(probs, part) - dot(pairs, part))).reshape(N_X, rows, CHUNK)
        dpf[:, :, columns(n)] = out
        dps[:, :, columns(n)] = out.astype(BF)
        return carry

    lax.fori_loop(0, chunks, passage_terms, 0)
    dp_across = remote(dps.at[(1 - yh) * 2 + 1 - core], dpc_in.at[1], S_DP, blk=other_core)
    dp_here = remote(dps.at[yh * 2 + 1 - core], dpc_in.at[0], S_DP + 1, blk=other_core)
    dp_across.start()
    dp_here.start()
    dp_across.wait_recv()

    def sum_across(n, carry):
        dpy[:, columns(n)] = (dpf[across, :, columns(n)] + dpc_in[1, :, columns(n)].astype(F32)).astype(BF)
        return carry

    lax.fori_loop(0, chunks, sum_across, 0)
    dp_y = remote(dpy, dpy_in, S_DP + 2, blk=other_yh)
    dp_y.start()
    pp_copies = ring_second(pp_copies, pps, pp_pass, pp_sum, pp_in, S_PP)

    loss_col = lse_col - own_column(picked)
    loss_out[...] = jnp.sum(jnp.where(eye, loss_col, 0.0), axis=0, keepdims=True)
    for copy in (*t_copies[2:], *pp_copies[2:]):
        copy.wait_recv()

    def query_sum(n, carry):
        terms = tf[x, :, columns(n)]
        paired_rows = pps[x, :, columns(n)].astype(F32)
        for side in range(2):
            terms = terms + t_in[side, :, columns(n)].astype(F32)
            paired_rows = paired_rows + pp_in[side, :, columns(n)].astype(F32)
        hard = neg[:, columns(n)].astype(F32) - paired_rows
        qd_out[:, columns(n)] = (SCALE * (alpha_col * terms + hard_weight_col * hard)).astype(BF)
        return carry

    lax.fori_loop(0, chunks, query_sum, 0)

    each_partner(lambda t: weight(t).wait_recv())
    hw_in[pl.ds(pl.multiple_of(dp * 8, 8), 8), :] = hw[pl.ds(pl.multiple_of(dp * 8, 8), 8), :]
    hard_high, hard_low = split(by_asked(hw_in[every_8th, :]).T)

    def widen_q(t):
        push(t).wait_recv()
        widen(qscr, qrecv, Q_ROWS, dp_peer(t)[1])

    widen(qscr, qrecv, Q_ROWS, dp)
    each_partner(widen_q)
    gather_rows(qn, place_q)
    dp_here.wait_recv()
    dp_y.wait_recv()

    def passage_sum(n, carry):
        terms = qn[:, columns(n)]
        out = dpf[mine, :, columns(n)] + SCALE * (dot(hard_high, terms) + dot(hard_low, terms))
        out = out + dpc_in[0, :, columns(n)].astype(F32) + dpy_in[:, columns(n)].astype(F32)
        pg_out[:, columns(n)] = out.astype(BF)
        return carry

    lax.fori_loop(0, chunks, passage_sum, 0)

    for copy in (q_right, q_left, q_on, q_back, p_core, p_across, p_pass, *st_copies, *t_copies, *pp_copies, *al_copies):
        copy.wait_send()
    for copy in (dp_across, dp_here, dp_y):
        copy.wait_send()

    def sent(t):
        request(t).wait_send()
        fetch(t).wait_send()
        push(t).wait_send()
        weight(t).wait_send()

    each_partner(sent)


def shards(queries, passages, positive, hard_owner, hard_slot):
    q, p = queries[0], passages[0]
    rows, width = q.shape
    wide = N_X * rows
    vmem = pl.BlockSpec(memory_space=pltpu.VMEM)
    anywhere = pl.BlockSpec(memory_space=pl.ANY)
    block, halves = (rows, width), (rows, width // 2)
    loss, qd, pg = pl.pallas_call(
        kernel,
        out_shape=(pltpu.VMEM((1, rows), F32), pltpu.VMEM(block, BF), pltpu.VMEM(block, BF)),
        in_specs=[vmem] * 3 + [anywhere] * 2,
        out_specs=[vmem] * 3,
        scratch_shapes=[
            pltpu.VMEM((N_X, *block), BF),
            pltpu.VMEM((N_X, *block), BF),
            pltpu.VMEM((N_DP * P_ROWS, LANES), F32),
            pltpu.VMEM((N_DP * Q_ROWS, LANES), F32),
            pltpu.VMEM((N_DP, P_ROWS, LANES), BF),
            pltpu.VMEM((N_DP, Q_ROWS, LANES), BF),
            pltpu.VMEM((N_DP, P_ROWS, LANES), BF),
            pltpu.VMEM((N_DP, Q_ROWS, LANES), BF),
            pltpu.VMEM((N_DP * CAP, width), BF),
            pltpu.VMEM((N_DP * CAP, width), BF),
            pltpu.VMEM(block, BF),
            pltpu.VMEM((N_DP * 8, LANES), F32),
            pltpu.VMEM((N_DP * 8, LANES), F32),
            pltpu.VMEM((N_DP * 8, LANES), F32),
            pltpu.VMEM((N_DP * 8, LANES), F32),
            pltpu.VMEM((8, wide), F32),
            pltpu.VMEM((N_X, 8, wide), F32),
            pltpu.VMEM((8, wide), F32),
            pltpu.VMEM((N_X, 8, wide), F32),
            pltpu.VMEM((N_X, *block), F32),
            pltpu.VMEM((N_X, *block), BF),
            pltpu.VMEM((2, *block), BF),
            pltpu.VMEM((2, *halves), BF),
            pltpu.VMEM((2, *halves), BF),
            pltpu.VMEM((N_X, *block), BF),
            pltpu.VMEM((2, *block), BF),
            pltpu.VMEM((2, *halves), BF),
            pltpu.VMEM((2, *halves), BF),
            pltpu.VMEM((N_X, *block), F32),
            pltpu.VMEM((N_X, *block), BF),
            pltpu.VMEM((2, *block), BF),
            pltpu.VMEM(block, BF),
            pltpu.VMEM(block, BF),
            pltpu.SemaphoreType.DMA((N_SEM,)),
            pltpu.SemaphoreType.DMA((N_SEM,)),
            pltpu.SemaphoreType.DMA((2,)),
        ],
        compiler_params=pltpu.CompilerParams(
            collective_id=0, has_side_effects=True, vmem_limit_bytes=56 * 2**20
        ),
        cost_estimate=pl.CostEstimate(flops=3 * 10**9, bytes_accessed=2 * 10**6, transcendentals=2 * 10**5),
    )(positive, hard_owner.reshape(1, rows), hard_slot.reshape(1, rows), q, p)
    return loss, qd[None], pg[None]


def solution(mesh):
    placed = (
        P("dp", "blk", None),
        P("dp", "blk", None),
        P("dp", None),
        P("dp", "blk", None),
        P("dp", "blk", None),
    )
    return jax.shard_map(
        shards,
        mesh=mesh,
        in_specs=placed,
        out_specs=(P("dp", "blk"), P("dp", "blk", None), P("dp", "blk", None)),
        check_vma=False,
    )
```

time: 111 us -> 105 us (0.946)
  local copies, waits for them, and re-layouts: 5.23 us -> 2.05 us
  other arithmetic: 1.26 us -> 0 us
    unnamed x14 -> x3, local copies, waits for them, and re-layouts: 5.06 us -> 2.05 us
where the time goes in v2:
time: 105 us
  Pallas kernels  102 us (97%)
  local copies, waits for them, and re-layouts  2.05 us (2%)
    pallas_call x1, Pallas kernels, shards(): pl.pallas_call(kernel, out_shape=(pltpu.VMEM((1, rows), F32), pltpu.VMEM(...  102 us

profile of v2, /device:TPU:1, one launch (start us, length us, event | category | flops | bytes accessed | tf_op | source)
XLA Modules:
  0.0 105.1 jit_solution(17933334718131146392)
XLA Ops:
  0.6 102.4 %shard_map.76 = (f32[1,64]{1,0:T(1,128)S(1)}, bf16[64,3584]{1,0:T(8,128)(2,1)S(1)}, bf16[64,3584]{1,0:T(8,128)(2,1)S(1)}) custom-call(s32[1,1024]{1,0:T(1,128)} %positive.1, s32[1,64]{1,0:T(1,128)} %bitcast.10, s32[1,64]{1,0:T(1,128)} %bitcast.11, bf16[64,3584]{1,0:T(8,128)(2,1)} %bitcast.8, bf16[64,3584]{1,0:T(8,128)(2,1)} %bitcast.9), custom_call_target="tpu_custom_call" | custom-call | flops 3000000000 | bytes 2000000 | tf_op jit(solution)/shard_map/pallas_call | solution.py:477
  103.1 0.5 copy.11
  103.6 0.8 copy.12
  104.4 0.8 copy.13

commit v3 on v2

--- a/solution.py
+++ b/solution.py
@@ -390,27 +390,38 @@
     alpha = sum(alphas_in[i, 0:1, :] for i in range(N_X))
     probs = (weights * alpha).astype(BF)
 
+    size = half // chunks
+
+    def piece(n):
+        return pl.ds(pl.multiple_of(n * size, size), size)
+
     def passage_terms(n, carry):
-        part = qg[:, :, columns(n)].reshape(wide, CHUNK)
-        out = (SCALE * (dot(probs, part) - dot(pairs, part))).reshape(N_X, rows, CHUNK)
-        dpf[:, :, columns(n)] = out
-        dps[:, :, columns(n)] = out.astype(BF)
-        return carry
-
-    lax.fori_loop(0, chunks, passage_terms, 0)
-    dp_across = remote(dps.at[(1 - yh) * 2 + 1 - core], dpc_in.at[1], S_DP, blk=other_core)
-    dp_here = remote(dps.at[yh * 2 + 1 - core], dpc_in.at[0], S_DP + 1, blk=other_core)
-    dp_across.start()
+        part = qg[:, :, piece(n)].reshape(wide, size)
+        out = (SCALE * (dot(probs, part) - dot(pairs, part))).reshape(N_X, rows, size)
+        dpf[:, :, piece(n)] = out
+        dps[:, :, piece(n)] = out.astype(BF)
+        return carry
+
+    def sum_across(n, carry):
+        dpy[:, piece(n)] = (dpf[across, :, piece(n)] + dpc_in[1, :, piece(n)].astype(F32)).astype(BF)
+        return carry
+
+    dp_across, dp_y = [], []
+    for h, part_of in enumerate((low_half, high_half)):
+        lax.fori_loop(h * chunks, (h + 1) * chunks, passage_terms, 0)
+        copy = remote(
+            dps.at[(1 - yh) * 2 + 1 - core, :, part_of], dpc_in.at[1, :, part_of], S_DP + h, blk=other_core
+        )
+        copy.start()
+        dp_across.append(copy)
+    for h, part_of in enumerate((low_half, high_half)):
+        dp_across[h].wait_recv()
+        lax.fori_loop(h * chunks, (h + 1) * chunks, sum_across, 0)
+        copy = remote(dpy.at[:, part_of], dpy_in.at[:, part_of], S_DP + 2 + h, blk=other_yh)
+        copy.start()
+        dp_y.append(copy)
+    dp_here = remote(dps.at[yh * 2 + 1 - core], dpc_in.at[0], S_P + 3, blk=other_core)
     dp_here.start()
-    dp_across.wait_recv()
-
-    def sum_across(n, carry):
-        dpy[:, columns(n)] = (dpf[across, :, columns(n)] + dpc_in[1, :, columns(n)].astype(F32)).astype(BF)
-        return carry
-
-    lax.fori_loop(0, chunks, sum_across, 0)
-    dp_y = remote(dpy, dpy_in, S_DP + 2, blk=other_yh)
-    dp_y.start()
     pp_copies = ring_second(pp_copies, pps, pp_pass, pp_sum, pp_in, S_PP)
 
     loss_col = lse_col - own_column(picked)
@@ -442,7 +453,8 @@
     each_partner(widen_q)
     gather_rows(qn, place_q)
     dp_here.wait_recv()
-    dp_y.wait_recv()
+    for copy in dp_y:
+        copy.wait_recv()
 
     def passage_sum(n, carry):
         terms = qn[:, columns(n)]
@@ -455,7 +467,7 @@
 
     for copy in (q_right, q_left, q_on, q_back, p_core, p_across, p_pass, *st_copies, *t_copies, *pp_copies, *al_copies):
         copy.wait_send()
-    for copy in (dp_across, dp_here, dp_y):
+    for copy in (*dp_across, dp_here, *dp_y):
         copy.wait_send()
 
     def sent(t):

time: 105 us -> 105 us (level)
  no operation moved by 1% of the time
where the time goes in v3:
time: 105 us; the launch traced here: 104 us
  Pallas kernels  102 us (97%)
  local copies, waits for them, and re-layouts  2.05 us (2%)
    pallas_call x1, Pallas kernels, shards(): pl.pallas_call(kernel, out_shape=(pltpu.VMEM((1, rows), F32), pltpu.VMEM(...  102 us

profile of v3, /device:TPU:1, one launch (start us, length us, event | category | flops | bytes accessed | tf_op | source)
XLA Modules:
  0.0 104.4 jit_solution(5320343162300150575)
XLA Ops:
  0.6 101.7 %shard_map.76 = (f32[1,64]{1,0:T(1,128)S(1)}, bf16[64,3584]{1,0:T(8,128)(2,1)S(1)}, bf16[64,3584]{1,0:T(8,128)(2,1)S(1)}) custom-call(s32[1,1024]{1,0:T(1,128)} %positive.1, s32[1,64]{1,0:T(1,128)} %bitcast.10, s32[1,64]{1,0:T(1,128)} %bitcast.11, bf16[64,3584]{1,0:T(8,128)(2,1)} %bitcast.8, bf16[64,3584]{1,0:T(8,128)(2,1)} %bitcast.9), custom_call_target="tpu_custom_call" | custom-call | flops 3000000000 | bytes 2000000 | tf_op jit(solution)/shard_map/pallas_call | solution.py:489
  102.3 0.5 copy.11
  102.8 0.8 copy.12
  103.6 0.8 copy.13

commit v4 on v3

--- a/solution.py
+++ b/solution.py
@@ -445,6 +445,12 @@
     hw_in[pl.ds(pl.multiple_of(dp * 8, 8), 8), :] = hw[pl.ds(pl.multiple_of(dp * 8, 8), 8), :]
     hard_high, hard_low = split(by_asked(hw_in[every_8th, :]).T)
 
+    def sent_before(t):
+        request(t).wait_send()
+        fetch(t).wait_send()
+
+    each_partner(sent_before)
+
     def widen_q(t):
         push(t).wait_recv()
         widen(qscr, qrecv, Q_ROWS, dp_peer(t)[1])
@@ -471,8 +477,6 @@
         copy.wait_send()
 
     def sent(t):
-        request(t).wait_send()
-        fetch(t).wait_send()
         push(t).wait_send()
         weight(t).wait_send()
 

time: 105 us -> 104 us (level)
  no operation moved by 1% of the time
where the time goes in v4:
time: 104 us
  Pallas kernels  102 us (98%)
  local copies, waits for them, and re-layouts  2.05 us (2%)
    pallas_call x1, Pallas kernels, shards(): pl.pallas_call(kernel, out_shape=(pltpu.VMEM((1, rows), F32), pltpu.VMEM(...  102 us

profile of v4, /device:TPU:1, one launch (start us, length us, event | category | flops | bytes accessed | tf_op | source)
XLA Modules:
  0.0 104.3 jit_solution(13258731321588219986)
XLA Ops:
  0.6 101.6 %shard_map.76 = (f32[1,64]{1,0:T(1,128)S(1)}, bf16[64,3584]{1,0:T(8,128)(2,1)S(1)}, bf16[64,3584]{1,0:T(8,128)(2,1)S(1)}) custom-call(s32[1,1024]{1,0:T(1,128)} %positive.1, s32[1,64]{1,0:T(1,128)} %bitcast.10, s32[1,64]{1,0:T(1,128)} %bitcast.11, bf16[64,3584]{1,0:T(8,128)(2,1)} %bitcast.8, bf16[64,3584]{1,0:T(8,128)(2,1)} %bitcast.9), custom_call_target="tpu_custom_call" | custom-call | flops 3000000000 | bytes 2000000 | tf_op jit(solution)/shard_map/pallas_call | solution.py:493
  102.2 0.5 copy.11
  102.8 0.8 copy.12
  103.5 0.8 copy.13
